TPU v7x, 32 devices: a whole 2x2x4 slice. The times are simulated.
32 devices in a mesh: groups: 2 (over x), blk: 16 (over z, y, core).
Axes of the slice: x: 2, y: 2, z: 4, core: 2. Of those that a mesh axis runs over, the one named last changes fastest.
Arguments:
- queries: bfloat16 [32768, 1024], P(('groups', 'blk')), parts along dimension 0, may hold values from -2.5 to 2.5
- passages: bfloat16 [128, 256, 1024], P('blk', 'groups'), parts along dimension 1, may hold values from -12 to 12
- block_list: int32 [256, 4], P(('groups', 'blk')), parts along dimension 0, may hold values from 0 to 127, as said below
- pair_count: int32 [256], P(('groups', 'blk')), parts along dimension 0, may hold values from 1 to 4, 256 in all
- positive: int32 [32768], P(('groups', 'blk')), parts along dimension 0, may hold values from 0 to 511
Outputs:
- row_loss: float32 [32768], P(('groups', 'blk')), parts along dimension 0
- query_grad: bfloat16 [32768, 1024], P(('groups', 'blk')), parts along dimension 0
- passage_grad: bfloat16 [128, 256, 1024], P('blk', 'groups'), parts along dimension 1
There are 2 independent parts, one for each index of `groups`. A program takes and returns all parts, laid end to end along the dimension named above; each array names one. Nothing has to cross between parts.
Inputs may be any that keep to these rules, and one draw needn't show every extreme that they name: `block_list`: each row names 4 different passage blocks; the 8 rows of one index of blk (aligned runs of 8 rows) name exactly 8 different passage blocks in all, each of them in the same number of rows. `pair_count`: the 128 entries of one group sum to 256, and some entry of each group equals 4; the sum holds for each group separately, not over all groups together.
All inputs are finite; a program needn't handle non-finite values.
Results may differ from a plain program's by a relative error of at most 0.0039.
Values may be sent and summed in bfloat16 or wider, within the bound.
A program may use at most 128 MiB of HBM per device.

v0:
```python
import jax
import jax.numpy as jnp
from jax import lax
from jax.sharding import PartitionSpec as P

D = 1024
BLK = 128
NB = 4
DISTINCT = 8


def send_back(partial_value):
    return lax.all_to_all(partial_value, "blk", split_axis=0, concat_axis=1, tiled=True)


def body(queries, passages, block_list, pair_count, positive):
    qblocks_here = block_list.shape[0]
    listed = block_list.reshape(-1)
    pair_total = listed.shape[0]
    span_cols = NB * BLK
    ordered = jnp.sort(listed)
    fresh = jnp.concatenate([jnp.ones((1,), jnp.bool_), ordered[1:] != ordered[:-1]])
    rank_of = jnp.cumsum(fresh.astype(jnp.int32)) - 1
    wanted = jnp.full((DISTINCT,), -1, jnp.int32).at[rank_of].set(ordered)
    matches = listed[:, None] == wanted[None, :]
    slot_index = jnp.sum(
        matches.astype(jnp.int32) * jnp.arange(DISTINCT, dtype=jnp.int32)[None, :], axis=1
    )
    merge_table = matches.astype(jnp.float32)
    requests = lax.all_gather(jnp.maximum(wanted, 0), "blk", axis=0, tiled=True)
    served = passages[:, requests, :]
    fetched = lax.all_to_all(served, "blk", split_axis=1, concat_axis=0, tiled=True)
    candidates = fetched[:, slot_index, :].reshape(BLK, qblocks_here, NB, D)
    query_rows = queries.reshape(qblocks_here, BLK, D)
    scores = jnp.einsum(
        "grd,cgnd->grnc", query_rows, candidates, preferred_element_type=jnp.float32
    )
    scores = scores.reshape(qblocks_here, BLK, span_cols)
    columns = jnp.arange(span_cols, dtype=jnp.int32)
    live_limit = pair_count * BLK
    is_live = columns[None, None, :] < live_limit[:, None, None]
    target_slot = positive.reshape(qblocks_here, BLK) % live_limit[:, None]
    row_max = jnp.max(jnp.where(is_live, scores, -jnp.inf), axis=2, keepdims=True)
    weights = jnp.where(is_live, jnp.exp(scores - row_max), jnp.float32(0.0))
    row_sum = jnp.sum(weights, axis=2, keepdims=True)
    target = jnp.take_along_axis(scores, target_slot[:, :, None], axis=2)[:, :, 0]
    row_loss = row_max[:, :, 0] + jnp.log(row_sum[:, :, 0]) - target
    onehot = (columns[None, None, :] == target_slot[:, :, None]).astype(jnp.float32)
    grad_scores = (
        (weights / row_sum - onehot).astype(jnp.bfloat16).reshape(qblocks_here, BLK, NB, BLK)
    )
    contrib = jnp.einsum(
        "grnc,grd->cgnd", grad_scores, query_rows, preferred_element_type=jnp.float32
    )
    contrib = contrib.reshape(BLK, pair_total, D)
    partial_value = jnp.einsum("cpd,pk->ckd", contrib, merge_table, precision=lax.Precision.HIGHEST)
    query_grad = jnp.einsum(
        "grnc,cgnd->grd", grad_scores, candidates, preferred_element_type=jnp.float32
    ).astype(jnp.bfloat16)
    returned = send_back(partial_value)
    passage_grad = jnp.zeros(passages.shape, jnp.float32).at[:, requests, :].add(returned)
    return (row_loss.reshape(-1), query_grad.reshape(-1, D), passage_grad.astype(jnp.bfloat16))


def solution(mesh):
    return jax.shard_map(
        body,
        mesh=mesh,
        in_specs=(
            P(("groups", "blk"), None),
            P("blk", "groups", None),
            P(("groups", "blk"), None),
            P(("groups", "blk")),
            P(("groups", "blk")),
        ),
        out_specs=(P(("groups", "blk")), P(("groups", "blk"), None), P("blk", "groups", None)),
        check_vma=False,
    )
```

profile of v0, /device:TPU:15, one launch (start us, length us, event | category | flops | bytes accessed | tf_op | source)
XLA Modules:
  0.0 248.9 jit_solution(7454822869387522437)
XLA Ops:
  0.7 0.9 copy.39
  1.6 1.6 sort.15
  3.4 0.1 copy.40
  3.6 0.1 fusion.9
  3.7 1.2 dynamic-slice
  5.6 0.7 scatter_custom_fusion
  6.3 0.1 maximum_dynamic-update-slice_fusion
  6.4 7.9 %all-reduce = s32[128]{0:T(128)S(1)} all-reduce(s32[128]{0:T(128)S(1)} %maximum_dynamic-update-slice_fusion), channel_id=1, replica_groups=mesh['groups'=2,'blk'=16] {'blk'}, use_global_device_ids=true, to_apply=%add | all-reduce | flops 128 | bytes 1024
  14.3 7.5 %gather_fusion = bf16[128,8,1024]{2,0,1:T(8,128)(2,1)} fusion(bf16[8,128,1024]{2,1,0:T(8,128)(2,1)} %param.6, s32[1024]{0:T(1024)S(1)} %pad_clamp_fusion.1), kind=kCustom, calls=%fused_computation | custom fusion | bytes 4194816 | tf_op jit(solution)/shard_map/gather | solution.py:31
  21.8 4.1 %copy.41 = bf16[8,128,1024]{2,0,1:T(8,128)(2,1)} copy(bf16[8,128,1024]{2,1,0:T(8,128)(2,1)} %bitcast.88) | data formatting | bytes 4194304 | tf_op jit(solution)/shard_map/gather | solution.py:31
  25.8 9.4 %all-to-all-start = ((bf16[8,128,1024]{2,0,1:T(8,128)(2,1)}), bf16[8,128,1024]{2,0,1:T(8,128)(2,1)}, u32[]{:S(2)}, u32[]{:S(2)}) async-start(bf16[8,128,1024]{2,0,1:T(8,128)(2,1)} %copy.41), calls=%async_computation | async-start | bytes 4194304 | tf_op jit(solution)/shard_map/all_to_all | solution.py:32
  35.4 0.1 fusion.10
  35.7 0.2 add_select_fusion
  35.9 46.9 %all-to-all-done = bf16[8,128,1024]{2,0,1:T(8,128)(2,1)} async-done(((bf16[8,128,1024]{2,0,1:T(8,128)(2,1)}), bf16[8,128,1024]{2,0,1:T(8,128)(2,1)}, u32[]{:S(2)}, u32[]{:S(2)}) %all-to-all-start) | async-done | bytes 2097184 | tf_op jit(solution)/shard_map/all_to_all | solution.py:32
  82.8 3.0 %copy.43 = bf16[16,8,8,1024]{3,2,1,0:T(8,128)(2,1)S(1)} copy(bf16[16,8,8,1024]{3,1,2,0:T(8,128)(2,1)} %bitcast.5) | data formatting | bytes 4194304 | tf_op jit(solution)/shard_map/all_to_all | solution.py:32
  85.8 2.5 copy.47
  88.3 6.5 %gather_fusion.1 = bf16[32,128,1024]{2,1,0:T(8,128)(2,1)} fusion(bf16[128,8,1024]{2,0,1:T(8,128)(2,1)} %copy.47, s32[1024]{0:T(1024)S(1)} %pad_clamp_fusion), kind=kCustom, calls=%fused_computation.1 | custom fusion | bytes 16777344 | tf_op jit(solution)/shard_map/gather | solution.py:33
  94.8 4.8 %fusion.5 = (f32[8,128]{1,0:T(8,128)S(1)}, f32[8,128,4,128]{3,1,2,0:T(8,128)S(1)}) fusion(pred[8,4,128]{2,1,0:T(4,128)(4,1)S(1)} %broadcast_compare_fusion, bf16[128,8,4,1024]{3,0,2,1:T(8,128)(2,1)} %bitcast.85, bf16[8,128,1024,1]{2,1,3,0:T(8,128)(2,1)S(1)} %bitcast.80), kind=kOutput, calls=%fused_computation.11 | convolution fusion | flops 1074789376 | bytes 12591104 | tf_op jit(solution)/shard_map/grd,cgnd->grnc/dot_general | solution.py:35
  99.6 0.7 fusion.8
  100.3 2.5 fusion.23
  102.8 13.3 %fusion.2 = f32[128,8,1024]{2,1,0:T(8,128)} fusion(f32[128,32,1024]{2,0,1:T(8,128)S(1)} %bitcast.82, s32[32]{0:T(128)S(1)} %reshape.340, s32[8]{0:T(128)S(1)} %scatter_custom_fusion), kind=kOutput, calls=%fused_computation.8 | convolution fusion | flops 402653440 | bytes 20971680 | tf_op jit(solution)/shard_map/cpd,pk->ckd/dot_general | solution.py:56
  116.1 4.9 %all-to-all-start.1 = ((f32[128,8,1024]{2,1,0:T(8,128)}), f32[128,8,1024]{2,1,0:T(8,128)}, u32[]{:S(2)}, u32[]{:S(2)}) async-start(f32[128,8,1024]{2,1,0:T(8,128)} %fusion.2), calls=%async_computation.1 | async-start | bytes 8388608 | tf_op jit(solution)/shard_map/all_to_all | solution.py:13
  121.0 0.2 compare_select_fusion.2
  121.3 14.8 %gather_fusion.2 = f32[1024]{0:T(1024)S(1)} fusion(f32[8,128,512]{1,2,0:T(8,128)} %bitcast.83, s32[1024]{0:T(1024)S(1)} %fusion.14), kind=kCustom, calls=%fused_computation.2 | custom fusion | bytes 20480 | tf_op jit(solution)/shard_map/jit(take_along_axis)/gather | solution.py:46
  136.1 0.7 bitcast_subtract_fusion.1
  136.8 7.3 %bitcast_convert_fusion = bf16[8,128,1024]{2,1,0:T(8,128)(2,1)} fusion(bf16[128,8,4,1024]{3,0,2,1:T(8,128)(2,1)} %bitcast.86, f32[8,128,4,128]{3,1,2,0:T(8,128)} %copy-done.1, s32[8,128]{1,0:T(8,128)S(1)} %add_select_fusion, s32[4,128]{1,0:T(4,128)S(1)} %multiply_add_fusion, f32[8,128]{1,0:T(8,128)S(1)} %fusion.8, f32[8,128]{1,0:T(8,128)S(1)} %get-tuple-element.20, ...), kind=kOutput, calls=%fused_computation.7 | convolution fusion | flops 1078460416 | bytes 12601344 | tf_op jit(solution)/shard_map/grnc,cgnd->grd/dot_general | solution.py:57
  144.2 69.3 %all-to-all-done.1 = f32[128,8,1024]{2,1,0:T(8,128)} async-done(((f32[128,8,1024]{2,1,0:T(8,128)}), f32[128,8,1024]{2,1,0:T(8,128)}, u32[]{:S(2)}, u32[]{:S(2)}) %all-to-all-start.1) | async-done | bytes 4194336 | tf_op jit(solution)/shard_map/all_to_all | solution.py:13
  213.5 7.7 %copy.50 = f32[8,16,8,1024]{3,0,2,1:T(8,128)} copy(f32[8,16,8,1024]{3,2,0,1:T(8,128)} %bitcast.33) | data formatting | bytes 8388608 | tf_op jit(solution)/shard_map/all_to_all | solution.py:13
  221.2 2.5 %broadcast_in_dim.50 = f32[8,128,1024]{2,0,1:T(8,128)} broadcast(f32[]{:T(128)} %constant.47.clone.1), dimensions={} | broadcast | bytes 4194308 | tf_op jit(solution)/shard_map/broadcast_in_dim | solution.py:61
  223.7 20.2 %scatter_fusion = f32[8,128,1024]{2,0,1:T(8,128)} fusion(f32[8,128,1024]{2,0,1:T(8,128)} %broadcast_in_dim.50, s32[128]{0:T(128)S(1)} %compare_select_fusion.6, f32[128,8,1024]{2,1,0:T(8,128)} %bitcast.84), kind=kCustom, calls=%fused_computation.4 | custom fusion | flops 1048576 | bytes 12583424 | tf_op jit(solution)/shard_map/scatter-add | solution.py:61
  243.9 2.5 %convert_element_type.30 = bf16[8,128,1024]{2,0,1:T(8,128)(2,1)S(1)} convert(f32[8,128,1024]{2,0,1:T(8,128)} %scatter_fusion) | non-fusion elementwise | flops 1048576 | bytes 6291456 | tf_op jit(solution)/shard_map/convert_element_type | solution.py:62
  246.4 2.5 copy.51
  (28 shorter events, 0.7 us)
Async XLA Ops:
  0.6 94.2 %copy-start = (bf16[1024,1024]{1,0:T(8,128)(2,1)S(1)}, bf16[1024,1024]{1,0:T(8,128)(2,1)}, u32[]{:S(2)}) copy-start(bf16[1024,1024]{1,0:T(8,128)(2,1)} %param.5) | copy-start | bytes 6291460
  25.8 9.7 %copy-start.3 = (s32[8]{0:T(128)S(1)}, s32[8]{0:T(128)}, u32[]{:S(2)}) copy-start(s32[8]{0:T(128)} %param.8) | copy-start | bytes 100
  25.8 9.8 %copy-start.2 = (s32[1024]{0:T(1024)S(1)}, s32[1024]{0:T(1024)}, u32[]{:S(2)}) copy-start(s32[1024]{0:T(1024)} %param.9) | copy-start | bytes 12292
  25.8 57.0 %all-to-all-start = ((bf16[8,128,1024]{2,0,1:T(8,128)(2,1)}), bf16[8,128,1024]{2,0,1:T(8,128)(2,1)}, u32[]{:S(2)}, u32[]{:S(2)}) async-start(bf16[8,128,1024]{2,0,1:T(8,128)(2,1)} %copy.41), calls=%async_computation | async-start | bytes 4194304 | tf_op jit(solution)/shard_map/all_to_all | solution.py:32
  99.6 3.2 %copy-start.1 = (f32[8,128,4,128]{3,1,2,0:T(8,128)}, f32[8,128,4,128]{3,1,2,0:T(8,128)S(1)}, u32[]{:S(2)}) copy-start(f32[8,128,4,128]{3,1,2,0:T(8,128)S(1)} %get-tuple-element.21) | copy-start | bytes 6291460
  116.1 97.4 %all-to-all-start.1 = ((f32[128,8,1024]{2,1,0:T(8,128)}), f32[128,8,1024]{2,1,0:T(8,128)}, u32[]{:S(2)}, u32[]{:S(2)}) async-start(f32[128,8,1024]{2,1,0:T(8,128)} %fusion.2), calls=%async_computation.1 | async-start | bytes 8388608 | tf_op jit(solution)/shard_map/all_to_all | solution.py:13
where the time goes:
time: 250 us; the launch traced here: 249 us
  waiting for transfers between devices  116 us (46%)
  local copies, waits for them, and re-layouts  54.2 us (22%)
  matrix products  27.9 us (11%)
  other arithmetic  26.9 us (11%)
  starting transfers between devices  14.3 us (6%)
  blocking collectives  7.89 us (3%)
    all_to_all x1, waiting for transfers between devices, send_back(): lax.all_to_all(partial_value, 'blk', split_axis=0, concat_axis=1, tiled=T...  69.3 us
    all_to_all x1, waiting for transfers between devices, body(): lax.all_to_all(served, 'blk', split_axis=1, concat_axis=0, tiled=True)  46.9 us
    scatter-add x1, other arithmetic, body(): jnp.zeros(passages.shape, jnp.float32).at[:, requests, :].add(returned)  20.2 us
    gather x1, local copies, waits for them, and re-layouts, body(): jnp.take_along_axis(scores, target_slot[:, :, None], axis=2)[:, :, 0]  14.8 us
    dot_general x1, matrix products, body(): jnp.einsum('cpd,pk->ckd', contrib, merge_table, precision=lax.Precision.H...  13.3 us
    gather x2, local copies, waits for them, and re-layouts, body(): served = passages[:, requests, :]  11.6 us
    all_to_all x1, starting transfers between devices, body(): lax.all_to_all(served, 'blk', split_axis=1, concat_axis=0, tiled=True)  9.42 us
    unnamed x1, blocking collectives  7.89 us
  transfers between devices with their start and end apart: 2, of which 2 were waited for; matrix products, arithmetic and copies ran while one was open for 10% of the time, Pallas kernels for 0%

commit v1 on v0

--- a/solution.py
+++ b/solution.py
@@ -29,7 +29,19 @@
     merge_table = matches.astype(jnp.float32)
     requests = lax.all_gather(jnp.maximum(wanted, 0), "blk", axis=0, tiled=True)
     served = passages[:, requests, :]
-    fetched = lax.all_to_all(served, "blk", split_axis=1, concat_axis=0, tiled=True)
+    ways, here = (lax.axis_size("blk"), lax.axis_index("blk"))
+    width = served.shape[1] // ways
+    shape = list(served.shape)
+    shape[1] = width
+    height = shape[0]
+    shape[0] = height * ways
+    full = jnp.zeros(shape, served.dtype)
+    for mask in range(ways):
+        part = lax.dynamic_slice_in_dim(served, (here ^ mask) * width, width, axis=1)
+        if mask:
+            part = lax.ppermute(part, "blk", [(d, d ^ mask) for d in range(ways)])
+        full = lax.dynamic_update_slice_in_dim(full, part, (here ^ mask) * height, axis=0)
+    fetched = full
     candidates = fetched[:, slot_index, :].reshape(BLK, qblocks_here, NB, D)
     query_rows = queries.reshape(qblocks_here, BLK, D)
     scores = jnp.einsum(

time: 250 us -> 283 us (1.13)
  starting transfers between devices: 14.3 us -> 36.8 us
  local copies, waits for them, and re-layouts: 54.2 us -> 66.6 us
  waiting for transfers between devices: 116 us -> 111 us
  other arithmetic: 26.9 us -> 30.8 us
    all_to_all x1 -> x0, waiting for transfers between devices: 46.9 us -> none  [body(): lax.all_to_all(served, 'blk', split_axis=1, concat_axis=0, tiled=True)]
    ppermute x0 -> x15, waiting for transfers between devices: none -> 41.5 us  [body(): part = lax.ppermute(part, 'blk', [(d, d ^ mask) for d in range(ways)])]
    ppermute x0 -> x15, starting transfers between devices: none -> 28.6 us  [body(): part = lax.ppermute(part, 'blk', [(d, d ^ mask) for d in range(ways)])]
    dynamic_update_slice x0 -> x16, local copies, waits for them, and re-layouts: none -> 16.2 us  [body(): lax.dynamic_update_slice_in_dim(full, part, (here ^ mask) * height, axis=0)]
    all_to_all x1 -> x0, starting transfers between devices: 9.42 us -> none  [body(): lax.all_to_all(served, 'blk', split_axis=1, concat_axis=0, tiled=True)]
    all_to_all x2 -> x0, local copies, waits for them, and re-layouts: 5.47 us -> none  [body(): lax.all_to_all(served, 'blk', split_axis=1, concat_axis=0, tiled=True)]
    gather x2 -> x1, local copies, waits for them, and re-layouts: 11.6 us -> 7.51 us  [body(): served = passages[:, requests, :]]
    all_to_all x1, starting transfers between devices: 4.91 us -> 8.25 us  [send_back(): lax.all_to_all(partial_value, 'blk', split_axis=0, concat_axis=1, tiled=T...]
  transfers between devices with their start and end apart: 2 -> 16, of which waited for: 2 -> 11; matrix products, arithmetic and copies ran while one was open for 10% -> 15% of each run, Pallas kernels for 0% -> 0%
where the time goes in v1:
time: 283 us; the launch traced here: 282 us
  waiting for transfers between devices  111 us (39%)
  local copies, waits for them, and re-layouts  66.6 us (24%)
  starting transfers between devices  36.8 us (13%)
  other arithmetic  30.8 us (11%)
  matrix products  27.7 us (10%)
  blocking collectives  7.89 us (3%)
    all_to_all x1, waiting for transfers between devices, send_back(): lax.all_to_all(partial_value, 'blk', split_axis=0, concat_axis=1, tiled=T...  69.3 us
    ppermute x15, waiting for transfers between devices, body(): part = lax.ppermute(part, 'blk', [(d, d ^ mask) for d in range(ways)])  41.5 us
    ppermute x15, starting transfers between devices, body(): part = lax.ppermute(part, 'blk', [(d, d ^ mask) for d in range(ways)])  28.6 us
    scatter-add x1, other arithmetic, body(): jnp.zeros(passages.shape, jnp.float32).at[:, requests, :].add(returned)  20.1 us
    dynamic_update_slice x16, local copies, waits for them, and re-layouts, body(): lax.dynamic_update_slice_in_dim(full, part, (here ^ mask) * height, axis=0)  16.2 us
    gather x1, local copies, waits for them, and re-layouts, body(): jnp.take_along_axis(scores, target_slot[:, :, None], axis=2)[:, :, 0]  14.8 us
    dot_general x1, matrix products, body(): jnp.einsum('cpd,pk->ckd', contrib, merge_table, precision=lax.Precision.H...  13.1 us
    all_to_all x1, starting transfers between devices, send_back(): lax.all_to_all(partial_value, 'blk', split_axis=0, concat_axis=1, tiled=T...  8.25 us
  transfers between devices with their start and end apart: 16, of which 11 were waited for; matrix products, arithmetic and copies ran while one was open for 15% of the time, Pallas kernels for 0%

profile of v1, /device:TPU:15, one launch (start us, length us, event | category | flops | bytes accessed | tf_op | source)
XLA Modules:
  0.0 282.2 jit_solution(856831358326870708)
XLA Ops:
  7.5 7.9 %all-reduce = s32[128]{0:T(128)S(1)} all-reduce(s32[128]{0:T(128)S(1)} %get-tuple-element.32), channel_id=1, replica_groups=mesh['groups'=2,'blk'=16] {'blk'}, use_global_device_ids=true, to_apply=%add | all-reduce | flops 128 | bytes 1024
  16.0 7.5 %gather_fusion = bf16[128,8,1024]{2,0,1:T(8,128)(2,1)} fusion(bf16[8,128,1024]{2,1,0:T(8,128)(2,1)} %param.6, s32[1024]{0:T(1024)S(1)} %pad_clamp_fusion.1), kind=kCustom, calls=%fused_computation | custom fusion | bytes 4194816 | tf_op jit(solution)/shard_map/gather | solution.py:31
  23.5 2.6 dynamic-slice_bitcast_fusion
  26.1 3.9 %collective-permute-start.14 = (bf16[8,8,1024]{2,1,0:T(8,128)(2,1)S(1)}, bf16[8,8,1024]{2,1,0:T(8,128)(2,1)}, u32[]{:S(2)}, u32[]{:S(2)}) collective-permute-start(bf16[8,8,1024]{2,1,0:T(8,128)(2,1)S(1)} %get-tuple-element.12), channel_id=1, source_target_pairs={{0,15},{1,14},{2,13},{3,12},{4,11},{5,10},{6,9},{7,8},{8,7},{9,6},... | collective-permute-start | bytes 393224 | tf_op jit(solution)/shard_map/ppermute | solution.py:42
  43.0 6.4 %collective-permute-done.1 = bf16[8,8,1024]{2,1,0:T(8,128)(2,1)S(1)} collective-permute-done((bf16[8,8,1024]{2,1,0:T(8,128)(2,1)S(1)}, bf16[8,8,1024]{2,1,0:T(8,128)(2,1)S(1)}, u32[]{:S(2)}, u32[]{:S(2)}) %collective-permute-start.1) | collective-permute-done | bytes 131104 | tf_op jit(solution)/shard_map/ppermute | solution.py:42
  51.2 4.3 %collective-permute-done.2 = bf16[8,8,1024]{2,1,0:T(8,128)(2,1)S(1)} collective-permute-done((bf16[8,8,1024]{2,1,0:T(8,128)(2,1)S(1)}, bf16[8,8,1024]{2,1,0:T(8,128)(2,1)S(1)}, u32[]{:S(2)}, u32[]{:S(2)}) %collective-permute-start.2) | collective-permute-done | bytes 131104 | tf_op jit(solution)/shard_map/ppermute | solution.py:42
  57.2 3.0 %collective-permute-done.3 = bf16[8,8,1024]{2,1,0:T(8,128)(2,1)S(1)} collective-permute-done((bf16[8,8,1024]{2,1,0:T(8,128)(2,1)S(1)}, bf16[8,8,1024]{2,1,0:T(8,128)(2,1)S(1)}, u32[]{:S(2)}, u32[]{:S(2)}) %collective-permute-start.3) | collective-permute-done | bytes 131104 | tf_op jit(solution)/shard_map/ppermute | solution.py:42
  60.2 2.1 collective-permute-start.4
  63.0 3.4 %collective-permute-done.4 = bf16[8,8,1024]{2,1,0:T(8,128)(2,1)S(1)} collective-permute-done((bf16[8,8,1024]{2,1,0:T(8,128)(2,1)S(1)}, bf16[8,8,1024]{2,1,0:T(8,128)(2,1)S(1)}, u32[]{:S(2)}, u32[]{:S(2)}) %collective-permute-start.4) | collective-permute-done | bytes 131104 | tf_op jit(solution)/shard_map/ppermute | solution.py:42
  67.9 3.9 %collective-permute-done.5 = bf16[8,8,1024]{2,1,0:T(8,128)(2,1)S(1)} collective-permute-done((bf16[8,8,1024]{2,1,0:T(8,128)(2,1)S(1)}, bf16[8,8,1024]{2,1,0:T(8,128)(2,1)S(1)}, u32[]{:S(2)}, u32[]{:S(2)}) %collective-permute-start.5) | collective-permute-done | bytes 131104 | tf_op jit(solution)/shard_map/ppermute | solution.py:42
  71.8 2.1 collective-permute-start.6
  74.6 3.5 %collective-permute-done.6 = bf16[8,8,1024]{2,1,0:T(8,128)(2,1)S(1)} collective-permute-done((bf16[8,8,1024]{2,1,0:T(8,128)(2,1)S(1)}, bf16[8,8,1024]{2,1,0:T(8,128)(2,1)S(1)}, u32[]{:S(2)}, u32[]{:S(2)}) %collective-permute-start.6) | collective-permute-done | bytes 131104 | tf_op jit(solution)/shard_map/ppermute | solution.py:42
  80.1 5.2 %collective-permute-done.7 = bf16[8,8,1024]{2,1,0:T(8,128)(2,1)S(1)} collective-permute-done((bf16[8,8,1024]{2,1,0:T(8,128)(2,1)S(1)}, bf16[8,8,1024]{2,1,0:T(8,128)(2,1)S(1)}, u32[]{:S(2)}, u32[]{:S(2)}) %collective-permute-start.7) | collective-permute-done | bytes 131104 | tf_op jit(solution)/shard_map/ppermute | solution.py:42
  85.2 3.5 %collective-permute-start.8 = (bf16[8,8,1024]{2,1,0:T(8,128)(2,1)S(1)}, bf16[8,8,1024]{2,1,0:T(8,128)(2,1)S(1)}, u32[]{:S(2)}, u32[]{:S(2)}) collective-permute-start(bf16[8,8,1024]{2,1,0:T(8,128)(2,1)S(1)} %get-tuple-element.18), channel_id=1, source_target_pairs={{0,9},{1,8},{2,11},{3,10},{4,13},{5,12},{6,15},{7,14},{8,1},{9,0},... | collective-permute-start | bytes 393224 | tf_op jit(solution)/shard_map/ppermute | solution.py:42
  89.5 3.8 %collective-permute-done.8 = bf16[8,8,1024]{2,1,0:T(8,128)(2,1)S(1)} collective-permute-done((bf16[8,8,1024]{2,1,0:T(8,128)(2,1)S(1)}, bf16[8,8,1024]{2,1,0:T(8,128)(2,1)S(1)}, u32[]{:S(2)}, u32[]{:S(2)}) %collective-permute-start.8) | collective-permute-done | bytes 131104 | tf_op jit(solution)/shard_map/ppermute | solution.py:42
  93.2 3.9 %collective-permute-start.9 = (bf16[8,8,1024]{2,1,0:T(8,128)(2,1)S(1)}, bf16[8,8,1024]{2,1,0:T(8,128)(2,1)S(1)}, u32[]{:S(2)}, u32[]{:S(2)}) collective-permute-start(bf16[8,8,1024]{2,1,0:T(8,128)(2,1)S(1)} %get-tuple-element.17), channel_id=1, source_target_pairs={{0,10},{1,11},{2,8},{3,9},{4,14},{5,15},{6,12},{7,13},{8,2},{9,3},... | collective-permute-start | bytes 393224 | tf_op jit(solution)/shard_map/ppermute | solution.py:42
  97.9 4.2 %collective-permute-done.9 = bf16[8,8,1024]{2,1,0:T(8,128)(2,1)S(1)} collective-permute-done((bf16[8,8,1024]{2,1,0:T(8,128)(2,1)S(1)}, bf16[8,8,1024]{2,1,0:T(8,128)(2,1)S(1)}, u32[]{:S(2)}, u32[]{:S(2)}) %collective-permute-start.9) | collective-permute-done | bytes 131104 | tf_op jit(solution)/shard_map/ppermute | solution.py:42
  102.1 4.4 %collective-permute-start.10 = (bf16[8,8,1024]{2,1,0:T(8,128)(2,1)S(1)}, bf16[8,8,1024]{2,1,0:T(8,128)(2,1)S(1)}, u32[]{:S(2)}, u32[]{:S(2)}) collective-permute-start(bf16[8,8,1024]{2,1,0:T(8,128)(2,1)S(1)} %get-tuple-element.16), channel_id=1, source_target_pairs={{0,11},{1,10},{2,9},{3,8},{4,15},{5,14},{6,13},{7,12},{8,3},{9,2},... | collective-permute-start | bytes 393224 | tf_op jit(solution)/shard_map/ppermute | solution.py:42
  107.2 3.7 %collective-permute-done.10 = bf16[8,8,1024]{2,1,0:T(8,128)(2,1)S(1)} collective-permute-done((bf16[8,8,1024]{2,1,0:T(8,128)(2,1)S(1)}, bf16[8,8,1024]{2,1,0:T(8,128)(2,1)S(1)}, u32[]{:S(2)}, u32[]{:S(2)}) %collective-permute-start.10) | collective-permute-done | bytes 131104 | tf_op jit(solution)/shard_map/ppermute | solution.py:42
  118.2 6.8 %gather_fusion.1 = bf16[32,128,1024]{2,1,0:T(8,128)(2,1)} fusion(bf16[128,8,1024]{2,0,1:T(8,128)(2,1)} %copy_dynamic-update-slice_fusion, s32[1024]{0:T(1024)S(1)} %pad_clamp_fusion), kind=kCustom, calls=%fused_computation.1 | custom fusion | bytes 16777344 | tf_op jit(solution)/shard_map/gather | solution.py:45
  125.0 4.8 %fusion.5 = (f32[8,128]{1,0:T(8,128)S(1)}, f32[8,128,4,128]{3,1,2,0:T(8,128)S(1)}) fusion(pred[8,4,128]{2,1,0:T(4,128)(4,1)S(1)} %copy-done.6, bf16[128,8,4,1024]{3,0,2,1:T(8,128)(2,1)} %bitcast.112, bf16[8,128,1024,1]{2,1,3,0:T(8,128)(2,1)S(1)} %bitcast.107), kind=kOutput, calls=%fused_computation.11 | convolution fusion | flops 1074789376 | bytes 12591104 | tf_op jit(solution)/shard_map/grd,cgnd->grnc/dot_general | solution.py:47
  130.5 2.5 fusion.23
  133.0 13.1 %fusion.2 = f32[128,8,1024]{2,1,0:T(8,128)} fusion(f32[128,32,1024]{2,0,1:T(8,128)S(1)} %bitcast.109, s32[32]{0:T(128)S(1)} %copy-done.17, s32[8]{0:T(128)S(1)} %copy-done.19), kind=kOutput, calls=%fused_computation.8 | convolution fusion | flops 402653440 | bytes 20971680 | tf_op jit(solution)/shard_map/cpd,pk->ckd/dot_general | solution.py:68
  146.1 8.3 %all-to-all-start = ((f32[128,8,1024]{2,1,0:T(8,128)}), f32[128,8,1024]{2,1,0:T(8,128)}, u32[]{:S(2)}, u32[]{:S(2)}) async-start(f32[128,8,1024]{2,1,0:T(8,128)} %fusion.2), calls=%async_computation | async-start | bytes 8388608 | tf_op jit(solution)/shard_map/all_to_all | solution.py:13
  154.7 14.8 %gather_fusion.2 = f32[1024]{0:T(1024)S(1)} fusion(f32[8,128,512]{1,2,0:T(8,128)} %bitcast.110, s32[1024]{0:T(1024)S(1)} %fusion.14), kind=kCustom, calls=%fused_computation.2 | custom fusion | bytes 20480 | tf_op jit(solution)/shard_map/jit(take_along_axis)/gather | solution.py:58
  170.2 7.3 %bitcast_convert_fusion = bf16[8,128,1024]{2,1,0:T(8,128)(2,1)} fusion(bf16[128,8,4,1024]{3,0,2,1:T(8,128)(2,1)} %bitcast.113, f32[8,128,4,128]{3,1,2,0:T(8,128)} %copy-done.1, s32[8,128]{1,0:T(8,128)S(1)} %add_select_fusion, s32[4,128]{1,0:T(4,128)S(1)} %copy-done.9, f32[8,128]{1,0:T(8,128)S(1)} %fusion.8, f32[8,128]{1,0:T(8,128)S(1)} %get-tuple-element.30, ...), kind=kOutput, calls=%fused_computation.7 | convolution fusion | flops 1078460416 | bytes 12601344 | tf_op jit(solution)/shard_map/grnc,cgnd->grd/dot_general | solution.py:69
  177.6 69.3 %all-to-all-done = f32[128,8,1024]{2,1,0:T(8,128)} async-done(((f32[128,8,1024]{2,1,0:T(8,128)}), f32[128,8,1024]{2,1,0:T(8,128)}, u32[]{:S(2)}, u32[]{:S(2)}) %all-to-all-start) | async-done | bytes 4194336 | tf_op jit(solution)/shard_map/all_to_all | solution.py:13
  246.9 7.7 %copy.40 = f32[8,16,8,1024]{3,0,2,1:T(8,128)} copy(f32[8,16,8,1024]{3,2,0,1:T(8,128)} %bitcast.44) | data formatting | bytes 8388608 | tf_op jit(solution)/shard_map/all_to_all | solution.py:13
  254.6 2.5 broadcast_in_dim.54
  257.1 20.1 %scatter_fusion = f32[8,128,1024]{2,0,1:T(8,128)} fusion(f32[8,128,1024]{2,0,1:T(8,128)} %broadcast_in_dim.54, s32[128]{0:T(128)S(1)} %copy-done.15, f32[128,8,1024]{2,1,0:T(8,128)} %bitcast.111), kind=kCustom, calls=%fused_computation.4 | custom fusion | flops 1048576 | bytes 12583424 | tf_op jit(solution)/shard_map/scatter-add | solution.py:73
  277.2 2.5 convert_element_type.30
  279.7 2.5 copy.41
  (104 shorter events, 39.2 us)
Async XLA Ops:
  0.6 124.4 %copy-start = (bf16[1024,1024]{1,0:T(8,128)(2,1)S(1)}, bf16[1024,1024]{1,0:T(8,128)(2,1)}, u32[]{:S(2)}) copy-start(bf16[1024,1024]{1,0:T(8,128)(2,1)} %param.5) | copy-start | bytes 6291460
  1.7 33.2 %copy-start.16 = (s32[32]{0:T(128)}, s32[32]{0:T(128)S(1)}, u32[]{:S(2)}) copy-start(s32[32]{0:T(128)S(1)} %reshape.340) | copy-start | bytes 388
  6.3 28.6 %copy-start.18 = (s32[8]{0:T(128)}, s32[8]{0:T(128)S(1)}, u32[]{:S(2)}) copy-start(s32[8]{0:T(128)S(1)} %scatter_custom_fusion) | copy-start | bytes 100
  23.5 10.3 %copy-start.20 = (s32[8]{0:T(128)S(1)}, s32[8]{0:T(128)}, u32[]{:S(2)}) copy-start(s32[8]{0:T(128)} %param.8) | copy-start | bytes 100
  26.1 90.5 %collective-permute-start.14 = (bf16[8,8,1024]{2,1,0:T(8,128)(2,1)S(1)}, bf16[8,8,1024]{2,1,0:T(8,128)(2,1)}, u32[]{:S(2)}, u32[]{:S(2)}) collective-permute-start(bf16[8,8,1024]{2,1,0:T(8,128)(2,1)S(1)} %get-tuple-element.12), channel_id=1, source_target_pairs={{0,15},{1,14},{2,13},{3,12},{4,11},{5,10},{6,9},{7,8},{8,7},{9,6},... | collective-permute-start | bytes 393224 | tf_op jit(solution)/shard_map/ppermute | solution.py:42
  30.1 84.9 %collective-permute-start.13 = (bf16[8,8,1024]{2,1,0:T(8,128)(2,1)S(1)}, bf16[8,8,1024]{2,1,0:T(8,128)(2,1)}, u32[]{:S(2)}, u32[]{:S(2)}) collective-permute-start(bf16[8,8,1024]{2,1,0:T(8,128)(2,1)S(1)} %get-tuple-element.13), channel_id=1, source_target_pairs={{0,14},{1,15},{2,12},{3,13},{4,10},{5,11},{6,8},{7,9},{8,6},{9,7},... | collective-permute-start | bytes 393224 | tf_op jit(solution)/shard_map/ppermute | solution.py:42
  31.7 81.7 %collective-permute-start.12 = (bf16[8,8,1024]{2,1,0:T(8,128)(2,1)S(1)}, bf16[8,8,1024]{2,1,0:T(8,128)(2,1)}, u32[]{:S(2)}, u32[]{:S(2)}) collective-permute-start(bf16[8,8,1024]{2,1,0:T(8,128)(2,1)S(1)} %get-tuple-element.14), channel_id=1, source_target_pairs={{0,13},{1,12},{2,15},{3,14},{4,9},{5,8},{6,11},{7,10},{8,5},{9,4},... | collective-permute-start | bytes 393224 | tf_op jit(solution)/shard_map/ppermute | solution.py:42
  31.7 79.9 %collective-permute-start.11 = (bf16[8,8,1024]{2,1,0:T(8,128)(2,1)S(1)}, bf16[8,8,1024]{2,1,0:T(8,128)(2,1)}, u32[]{:S(2)}, u32[]{:S(2)}) collective-permute-start(bf16[8,8,1024]{2,1,0:T(8,128)(2,1)S(1)} %get-tuple-element.15), channel_id=1, source_target_pairs={{0,12},{1,13},{2,14},{3,15},{4,8},{5,9},{6,10},{7,11},{8,4},{9,5},... | collective-permute-start | bytes 393224 | tf_op jit(solution)/shard_map/ppermute | solution.py:42
  31.9 8.4 %collective-permute-start = (bf16[8,8,1024]{2,1,0:T(8,128)(2,1)}, bf16[8,8,1024]{2,1,0:T(8,128)(2,1)}, u32[]{:S(2)}, u32[]{:S(2)}) collective-permute-start(bf16[8,8,1024]{2,1,0:T(8,128)(2,1)} %get-tuple-element.26), channel_id=1, source_target_pairs={{0,1},{1,0},{2,3},{3,2},{4,5},{5,4},{6,7},{7,6},{8,9},{9,8},{10,11... | collective-permute-start | bytes 393224 | tf_op jit(solution)/shard_map/ppermute | solution.py:42
  36.2 3.8 %copy-start.7 = (s32[1024]{0:T(1024)S(1)}, s32[1024]{0:T(1024)}, u32[]{:S(2)}) copy-start(s32[1024]{0:T(1024)} %param.9) | copy-start | bytes 12292
  36.2 3.8 %copy-start.10 = (s32[8]{0:T(128)S(1)}, s32[8]{0:T(128)}, u32[]{:S(2)}) copy-start(s32[8]{0:T(128)} %get-tuple-element.29) | copy-start | bytes 100
  36.2 3.8 %copy-start.12 = (pred[8]{0:T(512)(128)(4,1)S(1)}, pred[8]{0:T(512)(128)(4,1)}, u32[]{:S(2)}) copy-start(pred[8]{0:T(512)(128)(4,1)} %broadcast_compare_fusion.1) | copy-start | bytes 28
  36.3 4.1 %copy-start.5 = (bf16[8,8,1024]{2,1,0:T(8,128)(2,1)S(1)}, bf16[8,8,1024]{2,1,0:T(8,128)(2,1)}, u32[]{:S(2)}) copy-start(bf16[8,8,1024]{2,1,0:T(8,128)(2,1)} %get-tuple-element.25) | copy-start | bytes 393220
  36.3 13.1 %copy-start.4 = (bf16[8,8,1024]{2,1,0:T(8,128)(2,1)S(1)}, bf16[8,8,1024]{2,1,0:T(8,128)(2,1)}, u32[]{:S(2)}) copy-start(bf16[8,8,1024]{2,1,0:T(8,128)(2,1)} %get-tuple-element.24) | copy-start | bytes 393220
  36.3 19.2 %copy-start.3 = (bf16[8,8,1024]{2,1,0:T(8,128)(2,1)S(1)}, bf16[8,8,1024]{2,1,0:T(8,128)(2,1)}, u32[]{:S(2)}) copy-start(bf16[8,8,1024]{2,1,0:T(8,128)(2,1)} %get-tuple-element.23) | copy-start | bytes 393220
  36.3 23.9 %copy-start.2 = (bf16[8,8,1024]{2,1,0:T(8,128)(2,1)S(1)}, bf16[8,8,1024]{2,1,0:T(8,128)(2,1)}, u32[]{:S(2)}) copy-start(bf16[8,8,1024]{2,1,0:T(8,128)(2,1)} %get-tuple-element.22) | copy-start | bytes 393220
  40.4 9.0 %collective-permute-start.1 = (bf16[8,8,1024]{2,1,0:T(8,128)(2,1)S(1)}, bf16[8,8,1024]{2,1,0:T(8,128)(2,1)S(1)}, u32[]{:S(2)}, u32[]{:S(2)}) collective-permute-start(bf16[8,8,1024]{2,1,0:T(8,128)(2,1)S(1)} %copy-done.5), channel_id=1, source_target_pairs={{0,2},{1,3},{2,0},{3,1},{4,6},{5,7},{6,4},{7,5},{8,10},{9,11},{10,... | collective-permute-start | bytes 393224 | tf_op jit(solution)/shard_map/ppermute | solution.py:42
  49.4 6.1 %collective-permute-start.2 = (bf16[8,8,1024]{2,1,0:T(8,128)(2,1)S(1)}, bf16[8,8,1024]{2,1,0:T(8,128)(2,1)S(1)}, u32[]{:S(2)}, u32[]{:S(2)}) collective-permute-start(bf16[8,8,1024]{2,1,0:T(8,128)(2,1)S(1)} %copy-done.4), channel_id=1, source_target_pairs={{0,3},{1,2},{2,1},{3,0},{4,7},{5,6},{6,5},{7,4},{8,11},{9,10},{10,... | collective-permute-start | bytes 393224 | tf_op jit(solution)/shard_map/ppermute | solution.py:42
  55.5 4.7 %collective-permute-start.3 = (bf16[8,8,1024]{2,1,0:T(8,128)(2,1)S(1)}, bf16[8,8,1024]{2,1,0:T(8,128)(2,1)S(1)}, u32[]{:S(2)}, u32[]{:S(2)}) collective-permute-start(bf16[8,8,1024]{2,1,0:T(8,128)(2,1)S(1)} %copy-done.3), channel_id=1, source_target_pairs={{0,4},{1,5},{2,6},{3,7},{4,0},{5,1},{6,2},{7,3},{8,12},{9,13},{10,... | collective-permute-start | bytes 393224 | tf_op jit(solution)/shard_map/ppermute | solution.py:42
  60.2 6.3 %collective-permute-start.4 = (bf16[8,8,1024]{2,1,0:T(8,128)(2,1)S(1)}, bf16[8,8,1024]{2,1,0:T(8,128)(2,1)S(1)}, u32[]{:S(2)}, u32[]{:S(2)}) collective-permute-start(bf16[8,8,1024]{2,1,0:T(8,128)(2,1)S(1)} %copy-done.2), channel_id=1, source_target_pairs={{0,5},{1,4},{2,7},{3,6},{4,1},{5,0},{6,3},{7,2},{8,13},{9,12},{10,... | collective-permute-start | bytes 393224 | tf_op jit(solution)/shard_map/ppermute | solution.py:42
  66.4 5.4 %collective-permute-start.5 = (bf16[8,8,1024]{2,1,0:T(8,128)(2,1)S(1)}, bf16[8,8,1024]{2,1,0:T(8,128)(2,1)S(1)}, u32[]{:S(2)}, u32[]{:S(2)}) collective-permute-start(bf16[8,8,1024]{2,1,0:T(8,128)(2,1)S(1)} %get-tuple-element.21), channel_id=1, source_target_pairs={{0,6},{1,7},{2,4},{3,5},{4,2},{5,3},{6,0},{7,1},{8,14},{9,15},{10,... | collective-permute-start | bytes 393224 | tf_op jit(solution)/shard_map/ppermute | solution.py:42
  71.8 6.3 %collective-permute-start.6 = (bf16[8,8,1024]{2,1,0:T(8,128)(2,1)S(1)}, bf16[8,8,1024]{2,1,0:T(8,128)(2,1)S(1)}, u32[]{:S(2)}, u32[]{:S(2)}) collective-permute-start(bf16[8,8,1024]{2,1,0:T(8,128)(2,1)S(1)} %get-tuple-element.20), channel_id=1, source_target_pairs={{0,7},{1,6},{2,5},{3,4},{4,3},{5,2},{6,1},{7,0},{8,15},{9,14},{10,... | collective-permute-start | bytes 393224 | tf_op jit(solution)/shard_map/ppermute | solution.py:42
  78.1 7.2 %collective-permute-start.7 = (bf16[8,8,1024]{2,1,0:T(8,128)(2,1)S(1)}, bf16[8,8,1024]{2,1,0:T(8,128)(2,1)S(1)}, u32[]{:S(2)}, u32[]{:S(2)}) collective-permute-start(bf16[8,8,1024]{2,1,0:T(8,128)(2,1)S(1)} %get-tuple-element.19), channel_id=1, source_target_pairs={{0,8},{1,9},{2,10},{3,11},{4,12},{5,13},{6,14},{7,15},{8,0},{9,1},... | collective-permute-start | bytes 393224 | tf_op jit(solution)/shard_map/ppermute | solution.py:42
  85.2 8.0 %collective-permute-start.8 = (bf16[8,8,1024]{2,1,0:T(8,128)(2,1)S(1)}, bf16[8,8,1024]{2,1,0:T(8,128)(2,1)S(1)}, u32[]{:S(2)}, u32[]{:S(2)}) collective-permute-start(bf16[8,8,1024]{2,1,0:T(8,128)(2,1)S(1)} %get-tuple-element.18), channel_id=1, source_target_pairs={{0,9},{1,8},{2,11},{3,10},{4,13},{5,12},{6,15},{7,14},{8,1},{9,0},... | collective-permute-start | bytes 393224 | tf_op jit(solution)/shard_map/ppermute | solution.py:42
  93.2 8.9 %collective-permute-start.9 = (bf16[8,8,1024]{2,1,0:T(8,128)(2,1)S(1)}, bf16[8,8,1024]{2,1,0:T(8,128)(2,1)S(1)}, u32[]{:S(2)}, u32[]{:S(2)}) collective-permute-start(bf16[8,8,1024]{2,1,0:T(8,128)(2,1)S(1)} %get-tuple-element.17), channel_id=1, source_target_pairs={{0,10},{1,11},{2,8},{3,9},{4,14},{5,15},{6,12},{7,13},{8,2},{9,3},... | collective-permute-start | bytes 393224 | tf_op jit(solution)/shard_map/ppermute | solution.py:42
  102.1 8.8 %collective-permute-start.10 = (bf16[8,8,1024]{2,1,0:T(8,128)(2,1)S(1)}, bf16[8,8,1024]{2,1,0:T(8,128)(2,1)S(1)}, u32[]{:S(2)}, u32[]{:S(2)}) collective-permute-start(bf16[8,8,1024]{2,1,0:T(8,128)(2,1)S(1)} %get-tuple-element.16), channel_id=1, source_target_pairs={{0,11},{1,10},{2,9},{3,8},{4,15},{5,14},{6,13},{7,12},{8,3},{9,2},... | collective-permute-start | bytes 393224 | tf_op jit(solution)/shard_map/ppermute | solution.py:42
  118.2 6.8 %copy-start.6 = (pred[8,4,128]{2,1,0:T(4,128)(4,1)S(1)}, pred[8,4,128]{2,1,0:T(4,128)(4,1)}, u32[]{:S(2)}) copy-start(pred[8,4,128]{2,1,0:T(4,128)(4,1)} %broadcast_compare_fusion) | copy-start | bytes 12292
  129.8 3.2 %copy-start.1 = (f32[8,128,4,128]{3,1,2,0:T(8,128)}, f32[8,128,4,128]{3,1,2,0:T(8,128)S(1)}, u32[]{:S(2)}) copy-start(f32[8,128,4,128]{3,1,2,0:T(8,128)S(1)} %get-tuple-element.31) | copy-start | bytes 6291460
  146.1 8.3 %copy-start.8 = (s32[1024]{0:T(1024)S(1)}, s32[1024]{0:T(1024)}, u32[]{:S(2)}) copy-start(s32[1024]{0:T(1024)} %param.9) | copy-start | bytes 12292
  146.1 8.3 %copy-start.11 = (s32[8]{0:T(128)S(1)}, s32[8]{0:T(128)}, u32[]{:S(2)}) copy-start(s32[8]{0:T(128)} %get-tuple-element.29) | copy-start | bytes 100
  146.1 8.3 %copy-start.13 = (pred[8]{0:T(512)(128)(4,1)S(1)}, pred[8]{0:T(512)(128)(4,1)}, u32[]{:S(2)}) copy-start(pred[8]{0:T(512)(128)(4,1)} %broadcast_compare_fusion.1) | copy-start | bytes 28
  146.1 100.7 %all-to-all-start = ((f32[128,8,1024]{2,1,0:T(8,128)}), f32[128,8,1024]{2,1,0:T(8,128)}, u32[]{:S(2)}, u32[]{:S(2)}) async-start(f32[128,8,1024]{2,1,0:T(8,128)} %fusion.2), calls=%async_computation | async-start | bytes 8388608 | tf_op jit(solution)/shard_map/all_to_all | solution.py:13
  (5 other events, 8.9 us)
